TPU v7x, 512 devices: a whole 4x4x16 slice. The times are simulated.
512 devices in a mesh: dx: 16 (over y, x), dy: 32 (over z, core).
Axes of the slice: x: 4, y: 4, z: 16, core: 2. Of those that a mesh axis runs over, the one named last changes fastest.
Arguments:
- audio: bfloat16 [32, 128, 2570], P('dy', 'dx'), may hold values from -6 to 6
- counts: int32 [32, 16], P('dy', 'dx'), may hold values from 1 to 8, 64 in all within a row
- cotangent: bfloat16 [32, 64, 256, 512], P('dy', 'dx'), may hold values from -6 to 6
- conv_first: bfloat16 [10, 512], replicated, may hold values from -2 to 2
- norm_gain: float32 [512], replicated, may hold values from 0.1 to 1.9
- norm_bias: float32 [512], replicated, may hold values from -3 to 3
- conv_second: bfloat16 [1536, 512], replicated, may hold values from -0.15625 to 0.15625
Outputs:
- grad_conv_first: float32 [10, 512], replicated
- grad_norm: float32 [2, 512], replicated
- grad_conv_second: float32 [1536, 512], P('dy')
Inputs may be any that keep to these rules, and one draw needn't show every extreme that they name: In each group along dy the counts sum to 64, and some device of each group holds exactly 8 live crops.
All inputs are finite; a program needn't handle non-finite values.
Results may differ from a plain program's by a relative error of at most 0.0051.
Values may be sent and summed in bfloat16 or wider, within the bound.
A program may use at most 128 MiB of HBM per device.

v0:
```python
import math
import jax
import jax.numpy as jnp
from jax import lax
from jax.sharding import PartitionSpec as P


def gelu_cdf(value):
    return 0.5 * (1.0 + lax.erf(value * 0.7071067811865476))


def gelu_slope(value):
    return gelu_cdf(value) + value * jnp.exp(-0.5 * value * value) * 0.3989422804014327


def forward_backward(
    crop_waves, cot_rows, conv_first, norm_gain, norm_bias, conv_second, loss_scale
):
    batch_size = crop_waves.shape[0]
    frames = cot_rows.shape[1]
    first_len = 2 * frames + 1
    channels = conv_second.shape[1]
    early_taps = crop_waves[:, : 5 * first_len].reshape(batch_size, first_len, 5)
    late_taps = crop_waves[:, 5 : 5 * first_len + 5].reshape(batch_size, first_len, 5)
    patches = jnp.concatenate([early_taps, late_taps], axis=2).reshape(batch_size * first_len, 10)
    pre_norm = jnp.dot(patches, conv_first, preferred_element_type=jnp.float32).reshape(
        batch_size, first_len, channels
    )
    centre = pre_norm - jnp.mean(pre_norm, axis=1, keepdims=True)
    inv_std = lax.rsqrt(jnp.mean(centre * centre, axis=1, keepdims=True) + 1e-05)
    normed = centre * inv_std
    shifted = normed * norm_gain + norm_bias
    hidden = (shifted * gelu_cdf(shifted)).astype(jnp.bfloat16)
    two_taps = hidden[:, : 2 * frames].reshape(batch_size, frames, 2 * channels)
    third_tap = hidden[:, 2::2]
    second_rows = jnp.concatenate([two_taps, third_tap], axis=2).reshape(
        batch_size * frames, 3 * channels
    )
    pre_act = jnp.dot(second_rows, conv_second, preferred_element_type=jnp.float32)
    grad_rows = (
        loss_scale
        * cot_rows.reshape(batch_size * frames, channels).astype(jnp.float32)
        * gelu_slope(pre_act)
    ).astype(jnp.bfloat16)
    grad_cols = jnp.dot(grad_rows, conv_second.T, preferred_element_type=jnp.float32).reshape(
        batch_size, frames, 3 * channels
    )
    first_taps = grad_cols[:, :, : 2 * channels].reshape(batch_size, 2 * frames, channels)
    late_tap = jnp.stack(
        [grad_cols[:, :, 2 * channels :], jnp.zeros((batch_size, frames, channels), jnp.float32)],
        axis=2,
    ).reshape(batch_size, 2 * frames, channels)
    grad_hidden = jnp.concatenate(
        [first_taps, jnp.zeros((batch_size, 1, channels), jnp.float32)], axis=1
    )
    grad_hidden = grad_hidden + jnp.concatenate(
        [jnp.zeros((batch_size, 2, channels), jnp.float32), late_tap[:, : 2 * frames - 1]], axis=1
    )
    grad_shift = grad_hidden * gelu_slope(shifted)
    gain_grad = jnp.sum(grad_shift * normed, axis=(0, 1))
    shift_grad = jnp.sum(grad_shift, axis=(0, 1))
    grad_scaled = grad_shift * norm_gain
    grad_pre = inv_std * (
        grad_scaled
        - jnp.mean(grad_scaled, axis=1, keepdims=True)
        - normed * jnp.mean(grad_scaled * normed, axis=1, keepdims=True)
    )
    grad_pre = grad_pre.astype(jnp.bfloat16).reshape(batch_size * first_len, channels)
    grad_first = jnp.dot(patches.T, grad_pre, preferred_element_type=jnp.float32)
    return (second_rows, grad_rows, grad_first, jnp.stack([gain_grad, shift_grad]))


def on_device(audio, counts, cotangent, conv_first, norm_gain, norm_bias, conv_second):
    groups = lax.axis_size("dx")
    position = lax.axis_index("dx")
    slot_count = audio.shape[1]
    receive = cotangent.shape[1]
    frames = cotangent.shape[2]
    all_counts = lax.all_gather(counts, "dx", axis=1, tiled=True)[0]
    starts = jnp.cumsum(all_counts, dtype=jnp.int32) - all_counts
    everything = lax.all_gather(audio, "dx", axis=1, tiled=True)[0]
    wanted = jnp.arange(receive, dtype=jnp.int32) * groups + position
    holder = (
        jnp.sum((starts[None, :] <= wanted[:, None]).astype(jnp.int32), axis=1, dtype=jnp.int32) - 1
    )
    offset = wanted - starts[holder]
    crop_waves = jnp.take(everything, holder * slot_count + offset, axis=0)
    loss_scale = 1.0 / math.sqrt(groups * lax.axis_size("dy") * receive * frames)
    second_rows, grad_rows, grad_first, grad_gains = forward_backward(
        crop_waves, cotangent[0], conv_first, norm_gain, norm_bias, conv_second, loss_scale
    )
    row_share = conv_second.shape[0] // lax.axis_size("dy")
    grad_second = jnp.dot(second_rows.T, grad_rows, preferred_element_type=jnp.float32)
    summed_first, summed_gains, whole_second = lax.psum(
        (grad_first, grad_gains, grad_second), ("dx", "dy")
    )
    summed_second = lax.dynamic_slice_in_dim(
        whole_second, lax.axis_index("dy") * row_share, row_share, 0
    )
    return (summed_first, summed_gains, summed_second)


def solution(mesh):
    in_specs = (P("dy", "dx", None), P("dy", "dx"), P("dy", "dx", None, None), P(), P(), P(), P())
    out_specs = (P(), P(), P("dy", None))
    return jax.shard_map(
        on_device, mesh=mesh, in_specs=in_specs, out_specs=out_specs, check_vma=False
    )
```

profile of v0, /device:TPU:2, one launch (start us, length us, event | category | flops | bytes accessed | tf_op | source)
XLA Modules:
  0.0 583.2 jit_solution(14442549444901075429)
XLA Ops:
  7.2 0.0 copy-start
  7.2 0.0 all-reduce.7.cloned.1.call-start
  8.0 1.3 dynamic-slice
  9.3 0.7 bitcast_dynamic-update-slice_fusion
  9.9 15.7 %all-reduce.3 = s32[16]{0:T(128)S(1)} all-reduce(s32[16]{0:T(128)S(1)} %bitcast_dynamic-update-slice_fusion), channel_id=1, replica_groups=mesh['dx'=16,'dy'=32] {'dx'}, use_global_device_ids=true, to_apply=%add.3 | all-reduce | flops 16 | bytes 128 | tf_op jit(solution)/shard_map/squeeze | solution.py:79
  25.6 0.1 copy.14
  25.7 0.1 reduce
  25.9 0.2 convert_reduce_fusion
  26.1 0.6 gather_fusion
  26.8 24.8 %all_gather.7 = bf16[1,128,2570]{2,1,0:T(8,128)(2,1)S(1)} all-gather(bf16[1,8,2570]{2,1,0:T(8,128)(2,1)} %param.7), channel_id=1, replica_groups=mesh['dx'=16,'dy'=32] {'dx'}, dimensions={1}, use_global_device_ids=true | all-gather | bytes 699040 | tf_op jit(solution)/shard_map/all_gather | solution.py:81
  51.5 0.6 gather_fusion.1
  52.1 0.1 broadcast_select_fusion
  52.2 0.1 fusion.26
  52.3 0.4 reshape.141
  52.7 0.3 copy.15
  53.0 0.4 reshape.142
  53.4 0.3 copy.16
  53.7 0.0 copy-start.5
  53.7 0.0 copy-start.6
  53.7 1.5 fusion.27
  55.2 0.0 copy-start.1
  55.2 0.6 multiply_reduce_fusion.2
  55.8 1.3 copy-done.1
  57.1 0.0 copy-done.5
  57.2 0.0 copy-done.6
  57.2 2.4 multiply_convert_fusion.1
  59.6 0.0 copy-start.3
  59.6 11.7 %slice.24 = bf16[4,256,512]{2,1,0:T(8,128)(2,1)} slice(bf16[4,513,512]{2,1,0:T(8,128)(2,1)} %multiply_convert_fusion.1), slice={[0:4:1], [2:513:2], [0:512:1]} | slice | bytes 2097152 | tf_op jit(solution)/shard_map/slice | solution.py:35
  71.2 3.1 slice.34
  74.3 0.0 copy-done.3
  74.3 1.6 convert_multiply_fusion
  75.9 4.1 concatenate.20
  80.0 0.0 copy-done
  80.0 0.0 copy-start.2
  80.0 0.0 copy-start.4
  80.0 5.1 fusion.11
  85.1 0.0 copy-done.2
  85.1 0.0 copy-done.4
  85.1 3.6 fusion.12
  88.6 0.0 all-reduce.7.cloned.1.call-update
  88.7 1.8 fusion.28
  90.5 1.5 slice.36
  92.0 2.4 slice.35
  94.4 4.9 reshape.144
  99.3 3.0 stack.15
  102.4 3.4 stack.16
  105.7 0.0 slice-start
  105.7 6.1 %reshape.145 = f32[4,512,512]{2,1,0:T(8,128)} reshape(f32[4,256,2,512]{3,2,1,0:T(2,128)} %stack.16) | data formatting | bytes 8388608 | tf_op jit(solution)/shard_map/reshape | solution.py:52
  111.8 0.0 slice-start.1
  111.8 7.3 %multiply_reduce_fusion = (f32[512]{0:T(512)S(1)}, f32[4,512]{1,0:T(4,128)S(1)}, f32[4,512]{1,0:T(4,128)S(1)}, f32[512]{0:T(512)S(1)}, f32[4,513,512]{2,1,0:T(8,128)S(1)}) fusion(f32[4,512]{1,0:T(4,128)S(1)} %add_rsqrt_fusion, f32[4,513,512]{2,1,0:T(8,128)} %copy-done.1, f32[4,512]{1,0:T(4,128)S(1)} %broadcast_multiply_fusion.2, f32[512]{0:T(512)S(1)} %copy-done.5, ...), kind=kLoop, calls=%fused_computation.8 | loop fusion | flops 22057984 | bytes 16826368 | tf_op jit(solution)/shard_map/reduce_sum | solution.py:60
  119.2 0.0 slice-done
  119.2 0.0 slice-done.1
  119.2 1.4 fusion.14
  120.6 105.0 %all-reduce.4 = (f32[10,512]{1,0:T(8,128)}, f32[2,512]{1,0:T(2,128)}) all-reduce(f32[10,512]{1,0:T(8,128)S(1)} %fusion.14, f32[2,512]{1,0:T(2,128)S(1)} %pad_maximum_fusion.8), channel_id=1, replica_groups=mesh['dx'=16,'dy'=32] {'dx','dy'}, use_global_device_ids=true, to_apply=%region_6.7 | all-reduce | flops 6144 | bytes 49152 | tf_op jit(solution)/shard_map/psum | solution.py:94
  225.6 349.2 %all-reduce.7.cloned.1.call-done = f32[1536,512]{1,0:T(8,128)} async-done(((f32[1536,512]{1,0:T(8,128)}), f32[1536,512]{1,0:T(8,128)}) %all-reduce.7.cloned.1.call-update) | async-done | bytes 3145744 | tf_op jit(solution)/shard_map/psum | solution.py:94
  574.9 1.5 constant_dynamic-slice_fusion
  (15 shorter events, 0.1 us)
Async XLA Ops:
  7.2 72.8 %copy-start = (bf16[1536,512]{1,0:T(8,128)(2,1)S(1)}, bf16[1536,512]{1,0:T(8,128)(2,1)}, u32[]{:S(2)}) copy-start(bf16[1536,512]{1,0:T(8,128)(2,1)} %param.13) | copy-start | bytes 4718596
  7.2 567.7 %all-reduce.7.cloned.1.call-start = ((), (), s32[]{:S(2)}) async-start(), calls=%async_computation | async-start | bytes 6291456 | tf_op jit(solution)/shard_map/psum | solution.py:94
  53.7 3.5 copy-start.5
  53.7 3.5 copy-start.6
  55.2 2.0 copy-start.1
  59.6 14.7 %copy-start.3 = (bf16[1,4,256,512]{3,2,1,0:T(8,128)(2,1)S(1)}, bf16[1,4,256,512]{3,2,1,0:T(8,128)(2,1)}, u32[]{:S(2)}) copy-start(bf16[1,4,256,512]{3,2,1,0:T(8,128)(2,1)} %param.9) | copy-start | bytes 3145732
  80.0 5.1 copy-start.2
  80.0 5.1 copy-start.4
  105.7 13.5 %slice-start = ((s8[4259840]{0:T(1024)(128)(4,1)}), s8[65536]{0:T(1024)(128)(4,1)S(1)}, s32[]{:S(2)}) async-start(s8[4259840]{0:T(1024)(128)(4,1)} %bitcast.48), calls=%async_computation.1 | async-start | bytes 131072
  111.8 7.4 %slice-start.1 = ((s8[4259840]{0:T(1024)(128)(4,1)}), s8[4194304]{0:T(1024)(128)(4,1)S(1)}, s32[]{:S(2)}) async-start(s8[4259840]{0:T(1024)(128)(4,1)} %bitcast.48), calls=%async_computation.2 | async-start | bytes 8388608
Sparse Core Ops, SparseCore 0:
  88.8 486.0 all-reduce.6
where the time goes:
time: 584 us; the launch traced here: 583 us
  waiting for transfers between devices  349 us (60%)
  blocking collectives  145 us (25%)
  local copies, waits for them, and re-layouts  47.7 us (8%)
  between operations  15 us (3%)
  matrix products  13.3 us (2%)
  other arithmetic  12.4 us (2%)
    psum x1, waiting for transfers between devices, on_device(): lax.psum((grad_first, grad_gains, grad_second), ('dx', 'dy'))  349 us
    psum x1, blocking collectives, on_device(): lax.psum((grad_first, grad_gains, grad_second), ('dx', 'dy'))  105 us
    all_gather x1, blocking collectives, on_device(): everything = lax.all_gather(audio, 'dx', axis=1, tiled=True)[0]  24.8 us
    squeeze x1, blocking collectives, on_device(): all_counts = lax.all_gather(counts, 'dx', axis=1, tiled=True)[0]  15.7 us
  transfers between devices with their start and end apart: 1, of which 1 were waited for; matrix products, arithmetic and copies ran while one was open for 5% of the time, Pallas kernels for 0%

commit v1 on v0

--- a/solution.py
+++ b/solution.py
@@ -92,7 +92,7 @@
     row_share = conv_second.shape[0] // lax.axis_size("dy")
     grad_second = jnp.dot(second_rows.T, grad_rows, preferred_element_type=jnp.float32)
     summed_first, summed_gains, whole_second = lax.psum(
-        (grad_first, grad_gains, grad_second), ("dx", "dy")
+        lax.psum((grad_first, grad_gains, grad_second), "dy"), "dx"
     )
     summed_second = lax.dynamic_slice_in_dim(
         whole_second, lax.axis_index("dy") * row_share, row_share, 0

time: 584 us -> 514 us (0.88)
  the two profiles are of different devices: /device:TPU:2 before, /device:TPU:32 now
where the time goes in v1:
time: 514 us; the launch traced here: 513 us
  waiting for transfers between devices  216 us (42%)
  blocking collectives  208 us (40%)
  local copies, waits for them, and re-layouts  47.7 us (9%)
  between operations  15 us (3%)
  matrix products  13.3 us (3%)
  other arithmetic  12.5 us (2%)
    psum x1, waiting for transfers between devices, on_device(): lax.psum((grad_first, grad_gains, grad_second), 'dy')  216 us
    psum x1, blocking collectives, on_device(): lax.psum((grad_first, grad_gains, grad_second), 'dy')  93.5 us
    psum x1, blocking collectives, on_device(): lax.psum(lax.psum((grad_first, grad_gains, grad_second), 'dy'), 'dx')  75.5 us
    all_gather x1, blocking collectives, on_device(): everything = lax.all_gather(audio, 'dx', axis=1, tiled=True)[0]  22.4 us
    squeeze x1, blocking collectives, on_device(): all_counts = lax.all_gather(counts, 'dx', axis=1, tiled=True)[0]  16.6 us
    slice x1, local copies, waits for them, and re-layouts, forward_backward(): third_tap = hidden[:, 2::2]  11.7 us
  transfers between devices with their start and end apart: 2, of which 1 were waited for; matrix products, arithmetic and copies ran while one was open for 6% of the time, Pallas kernels for 0%

profile of v1, /device:TPU:32, one launch (start us, length us, event | category | flops | bytes accessed | tf_op | source)
XLA Modules:
  0.0 513.0 jit_solution(1074078048316410719)
XLA Ops:
  7.2 0.0 copy-start
  7.2 0.0 all-reduce.9.cloned.1.call-start
  8.0 1.3 dynamic-slice
  9.3 0.7 bitcast_dynamic-update-slice_fusion
  9.9 16.6 %all-reduce.3 = s32[16]{0:T(128)S(1)} all-reduce(s32[16]{0:T(128)S(1)} %bitcast_dynamic-update-slice_fusion), channel_id=1, replica_groups=mesh['dx'=16,'dy'=32] {'dx'}, use_global_device_ids=true, to_apply=%add.3 | all-reduce | flops 16 | bytes 128 | tf_op jit(solution)/shard_map/squeeze | solution.py:79
  26.5 0.1 copy.14
  26.6 0.1 reduce
  26.8 0.2 convert_reduce_fusion
  27.0 0.6 gather_fusion
  27.7 22.4 %all_gather.7 = bf16[1,128,2570]{2,1,0:T(8,128)(2,1)S(1)} all-gather(bf16[1,8,2570]{2,1,0:T(8,128)(2,1)} %param.7), channel_id=1, replica_groups=mesh['dx'=16,'dy'=32] {'dx'}, dimensions={1}, use_global_device_ids=true | all-gather | bytes 699040 | tf_op jit(solution)/shard_map/all_gather | solution.py:81
  50.1 0.6 gather_fusion.1
  50.7 0.1 broadcast_select_fusion
  50.8 0.1 fusion.26
  50.8 0.4 reshape.141
  51.2 0.3 copy.15
  51.5 0.4 reshape.142
  51.9 0.3 copy.16
  52.2 0.0 copy-start.5
  52.2 0.0 copy-start.6
  52.2 1.5 fusion.27
  53.7 0.0 copy-start.1
  53.8 0.6 multiply_reduce_fusion.2
  54.3 1.3 copy-done.1
  55.7 0.0 copy-done.5
  55.7 0.0 copy-done.6
  55.7 2.4 multiply_convert_fusion.1
  58.1 0.0 copy-start.3
  58.1 11.7 %slice.24 = bf16[4,256,512]{2,1,0:T(8,128)(2,1)} slice(bf16[4,513,512]{2,1,0:T(8,128)(2,1)} %multiply_convert_fusion.1), slice={[0:4:1], [2:513:2], [0:512:1]} | slice | bytes 2097152 | tf_op jit(solution)/shard_map/slice | solution.py:35
  69.8 3.1 slice.34
  72.8 0.0 copy-done.3
  72.8 1.6 convert_multiply_fusion
  74.5 4.1 concatenate.20
  78.5 0.0 copy-done
  78.5 0.0 copy-start.2
  78.5 0.0 copy-start.4
  78.5 5.1 fusion.11
  83.6 0.0 copy-done.2
  83.6 0.0 copy-done.4
  83.6 3.6 fusion.12
  87.2 0.0 all-reduce.9.cloned.1.call-update
  87.2 0.2 all-reduce.11.cloned.1.call-start
  87.4 216.2 %all-reduce.9.cloned.1.call-done = f32[1536,512]{1,0:T(8,128)} async-done(((f32[1536,512]{1,0:T(8,128)}), f32[1536,512]{1,0:T(8,128)}) %all-reduce.9.cloned.1.call-update) | async-done | bytes 3145744 | tf_op jit(solution)/shard_map/psum | solution.py:95
  303.7 0.0 all-reduce.11.cloned.1.call-update
  303.7 1.8 fusion.28
  305.5 1.5 slice.36
  307.0 2.4 slice.35
  309.4 4.9 reshape.144
  314.4 3.0 stack.15
  317.4 3.4 stack.16
  320.8 0.0 slice-start
  320.8 6.1 %reshape.145 = f32[4,512,512]{2,1,0:T(8,128)} reshape(f32[4,256,2,512]{3,2,1,0:T(2,128)} %stack.16) | data formatting | bytes 8388608 | tf_op jit(solution)/shard_map/reshape | solution.py:52
  326.9 0.0 slice-start.1
  326.9 7.4 %multiply_reduce_fusion = (f32[512]{0:T(512)S(1)}, f32[4,512]{1,0:T(4,128)S(1)}, f32[4,512]{1,0:T(4,128)S(1)}, f32[512]{0:T(512)S(1)}, f32[4,513,512]{2,1,0:T(8,128)S(1)}) fusion(f32[4,512]{1,0:T(4,128)S(1)} %add_rsqrt_fusion, f32[4,513,512]{2,1,0:T(8,128)} %copy-done.1, f32[4,512]{1,0:T(4,128)S(1)} %broadcast_multiply_fusion.2, f32[512]{0:T(512)S(1)} %copy-done.5, ...), kind=kLoop, calls=%fused_computation.8 | loop fusion | flops 22057984 | bytes 16826368 | tf_op jit(solution)/shard_map/reduce_sum | solution.py:60
  334.3 0.0 slice-done
  334.3 0.0 slice-done.1
  334.3 1.4 fusion.14
  335.7 93.5 %all-reduce.4 = (f32[10,512]{1,0:T(8,128)S(1)}, f32[2,512]{1,0:T(2,128)S(1)}) all-reduce(f32[10,512]{1,0:T(8,128)S(1)} %fusion.14, f32[2,512]{1,0:T(2,128)S(1)} %pad_maximum_fusion.8), channel_id=1, replica_groups=mesh['dx'=16,'dy'=32] {'dy'}, use_global_device_ids=true, to_apply=%region_6.7 | all-reduce | flops 6144 | bytes 49152 | tf_op jit(solution)/shard_map/psum | solution.py:95
  429.2 75.5 %all-reduce.5 = (f32[10,512]{1,0:T(8,128)}, f32[2,512]{1,0:T(2,128)}) all-reduce(f32[10,512]{1,0:T(8,128)S(1)} %get-tuple-element.7, f32[2,512]{1,0:T(2,128)S(1)} %get-tuple-element.8), channel_id=1, replica_groups=mesh['dx'=16,'dy'=32] {'dx'}, use_global_device_ids=true, to_apply=%region_7.8 | all-reduce | flops 6144 | bytes 49152 | tf_op jit(solution)/shard_map/psum | solution.py:94
  504.6 0.0 all-reduce.11.cloned.1.call-done
  504.6 1.5 constant_dynamic-slice_fusion
  (15 shorter events, 0.1 us)
Async XLA Ops:
  7.2 71.4 %copy-start = (bf16[1536,512]{1,0:T(8,128)(2,1)S(1)}, bf16[1536,512]{1,0:T(8,128)(2,1)}, u32[]{:S(2)}) copy-start(bf16[1536,512]{1,0:T(8,128)(2,1)} %param.13) | copy-start | bytes 4718596
  7.2 296.5 %all-reduce.9.cloned.1.call-start = ((), (), s32[]{:S(2)}) async-start(), calls=%async_computation | async-start | bytes 6291456 | tf_op jit(solution)/shard_map/psum | solution.py:95
  52.2 3.5 copy-start.5
  52.2 3.5 copy-start.6
  53.7 2.0 copy-start.1
  58.1 14.7 %copy-start.3 = (bf16[1,4,256,512]{3,2,1,0:T(8,128)(2,1)S(1)}, bf16[1,4,256,512]{3,2,1,0:T(8,128)(2,1)}, u32[]{:S(2)}) copy-start(bf16[1,4,256,512]{3,2,1,0:T(8,128)(2,1)} %param.9) | copy-start | bytes 3145732
  78.5 5.1 copy-start.2
  78.5 5.1 copy-start.4
  87.2 417.4 %all-reduce.11.cloned.1.call-start = ((), (), s32[]{:S(2)}) async-start(), calls=%async_computation.1 | async-start | bytes 6291456 | tf_op jit(solution)/shard_map/psum | solution.py:94
  320.8 13.5 %slice-start = ((s8[4259840]{0:T(1024)(128)(4,1)}), s8[65536]{0:T(1024)(128)(4,1)S(1)}, s32[]{:S(2)}) async-start(s8[4259840]{0:T(1024)(128)(4,1)} %bitcast.48), calls=%async_computation.2 | async-start | bytes 131072
  326.9 7.4 %slice-start.1 = ((s8[4259840]{0:T(1024)(128)(4,1)}), s8[4194304]{0:T(1024)(128)(4,1)S(1)}, s32[]{:S(2)}) async-start(s8[4259840]{0:T(1024)(128)(4,1)} %bitcast.48), calls=%async_computation.3 | async-start | bytes 8388608
Sparse Core Ops, SparseCore 0:
  87.3 216.2 all-reduce.8
  307.4 128.9 all-reduce.10
